TPU v7x, 512 devices: a whole 4x4x16 slice. The times are simulated.
512 devices in a mesh: width: 16 (over y, z_hi), hidden: 32 (over x, z_lo, core).
Axes of the slice: x: 4, y: 4, z: 16 (z_hi: 4, z_lo: 4; z = z_hi * 4 + z_lo), core: 2. Of those that a mesh axis runs over, the one named last changes fastest.
Arguments:
- tokens: bfloat16 [384, 12288], P('hidden', 'width'), may hold values from -8 to 8
- gate_weight: bfloat16 [12288, 28672], P('width', 'hidden'), may hold values from -0.0546875 to 0.0546875
- up_weight: bfloat16 [12288, 28672], P('width', 'hidden'), may hold values from -0.0546875 to 0.0546875
- down_weight: bfloat16 [28672, 12288], P('hidden', 'width'), may hold values from -0.03125 to 0.03125
Outputs:
- block_out: bfloat16 [384, 12288], P('hidden', 'width')
All inputs are finite; a program needn't handle non-finite values.
Results may differ from a plain program's by a relative error of at most 0.0036.
Values may be sent and summed in bfloat16 or wider, within the bound.
A program may use at most 64 MiB of HBM per device.

v0:
```python
import jax
import jax.numpy as jnp
from jax import lax
from jax.sharding import PartitionSpec as P


def saturate(values, peak):
    level = 0.5 * (peak + 1e-06)
    return level * jnp.tanh(values / level)


def on_device(tokens, gate_weight, up_weight, down_weight):
    inputs = tokens.astype(jnp.float32)
    peak_in = lax.pmax(jnp.max(jnp.abs(inputs)), ("width", "hidden"))
    source = saturate(inputs, peak_in).astype(jnp.bfloat16)
    gathered = lax.all_gather(source, "hidden", axis=0, tiled=True)
    gate_part = jnp.dot(gathered, gate_weight, preferred_element_type=jnp.float32)
    up_part = jnp.dot(gathered, up_weight, preferred_element_type=jnp.float32)
    gate, up = lax.psum((gate_part, up_part), "width")
    act = jax.nn.silu(gate) * up
    peak_act = lax.pmax(jnp.max(jnp.abs(act)), "hidden")
    scaled_act = saturate(act, 0.125 * peak_act).astype(jnp.bfloat16)
    down = lax.psum_scatter(
        jnp.dot(scaled_act, down_weight, preferred_element_type=jnp.float32),
        "hidden",
        scatter_dimension=0,
        tiled=True,
    )
    return (inputs + down).astype(jnp.bfloat16)


def solution(mesh):
    in_specs = (
        P("hidden", "width"),
        P("width", "hidden"),
        P("width", "hidden"),
        P("hidden", "width"),
    )
    out_specs = P("hidden", "width")
    return jax.shard_map(
        on_device, mesh=mesh, in_specs=in_specs, out_specs=out_specs, check_vma=False
    )
```

profile of v0, /device:TPU:1, one launch (start us, length us, event | category | flops | bytes accessed | tf_op | source)
XLA Modules:
  0.0 647.7 jit_solution(4837040450884705808)
XLA Ops:
  6.5 0.0 copy-start
  6.5 0.0 all-reduce.5.cloned.1.call-start
  6.5 1.5 fusion.3
  8.0 111.0 %pmax.14 = f32[]{:T(128)} all-reduce(f32[]{:T(128)} %fusion.3), channel_id=1, replica_groups=mesh['width'=16,'hidden'=32] {'width','hidden'}, use_global_device_ids=true, to_apply=%region_1.0 | all-reduce | flops 1 | bytes 8 | tf_op jit(solution)/shard_map/pmax | solution.py:14
  119.7 0.8 fusion.8
  120.4 42.5 %all-gather = bf16[32,12,768]{2,1,0:T(8,128)(2,1)S(1)} all-gather(bf16[1,12,768]{2,1,0:T(8,128)(2,1)S(1)} %fusion.8), channel_id=1, replica_groups=mesh['width'=16,'hidden'=32] {'hidden'}, dimensions={0}, use_global_device_ids=true | all-gather | bytes 608256 | tf_op jit(solution)/shard_map/all_gather | solution.py:16
  162.9 0.1 reshape.1
  163.0 0.0 copy-done
  163.0 0.0 copy-start.1
  163.1 1.8 fusion.10
  164.9 0.0 copy-done.1
  164.9 1.9 fusion.9
  166.8 0.0 all-reduce.5.cloned.1.call-update
  166.8 294.8 %all-reduce.5.cloned.1.call-done = (f32[384,896]{1,0:T(8,128)}, f32[384,896]{1,0:T(8,128)}) async-done(((f32[384,896]{1,0:T(8,128)}, f32[384,896]{1,0:T(8,128)}), (f32[384,896]{1,0:T(8,128)}, f32[384,896]{1,0:T(8,128)})) %all-reduce.5.cloned.1.call-update) | async-done | bytes 2752528 | tf_op jit(solution)/shard_map/psum | solution.py:19
  461.6 0.0 copy-start.2
  461.6 2.8 abs_reduce_fusion
  464.4 70.6 %pmax.15 = f32[]{:T(128)} all-reduce(f32[]{:T(128)} %abs_reduce_fusion), channel_id=1, replica_groups=mesh['width'=16,'hidden'=32] {'hidden'}, use_global_device_ids=true, to_apply=%region_5.6 | all-reduce | flops 1 | bytes 8 | tf_op jit(solution)/shard_map/pmax | solution.py:21
  535.7 0.0 copy-done.2
  535.7 3.9 fusion.1
  539.5 0.0 copy-start.3
  539.5 77.4 %fusion = f32[16,768]{1,0:T(8,128)S(1)} fusion(f32[384,768]{1,0:T(8,128)} %fusion.1), kind=kCustom, calls=%all-reduce-scatter | all-reduce-scatter fusion | flops 393217 | bytes 1230848
  616.9 1.9 collective-permute-start
  618.8 1.3 collective-permute-start.1
  620.2 1.3 collective-permute-start.7
  621.5 1.3 collective-permute-start.2
  622.8 1.3 collective-permute-start.3
  624.1 0.0 collective-permute-done.7
  624.1 1.3 collective-permute-start.4
  625.4 0.0 collective-permute-done
  625.4 9.3 %collective-permute-start.5 = (f32[16,768]{1,0:T(8,128)S(1)}, f32[16,768]{1,0:T(8,128)S(1)}, u32[]{:S(2)}, u32[]{:S(2)}) collective-permute-start(f32[16,768]{1,0:T(8,128)S(1)} %fusion), channel_id=1, source_target_pairs={{0,6},{1,7},{2,8},{3,9},{4,10},{5,11},{6,12},{7,13},{8,14},{9,15},... | collective-permute-start | bytes 147464
  634.7 0.0 collective-permute-done.1
  634.7 2.5 collective-permute-start.6
  637.2 1.3 dynamic-slice.4
  639.2 0.0 collective-permute-done.2
  639.2 0.0 collective-permute-done.3
  639.2 0.0 collective-permute-done.4
  639.2 0.0 collective-permute-done.5
  639.2 0.0 collective-permute-done.6
  639.2 1.0 concatenate
  640.3 0.0 copy-done.3
  640.3 0.6 fusion.7
  (1 shorter events, 0.0 us)
Async XLA Ops:
  6.5 156.5 %copy-start = (bf16[768,896]{1,0:T(8,128)(2,1)S(1)}, bf16[768,896]{1,0:T(8,128)(2,1)}, u32[]{:S(2)}) copy-start(bf16[768,896]{1,0:T(8,128)(2,1)} %param.6) | copy-start | bytes 4128772
  6.5 455.0 %all-reduce.5.cloned.1.call-start = ((), (), s32[]{:S(2)}) async-start(), calls=%async_computation | async-start | bytes 5505024 | tf_op jit(solution)/shard_map/psum | solution.py:19
  163.0 1.9 copy-start.1
  461.6 74.1 %copy-start.2 = (f32[384,896]{1,0:T(8,128)S(1)}, f32[384,896]{1,0:T(8,128)}, u32[]{:S(2)}) copy-start(f32[384,896]{1,0:T(8,128)} %get-tuple-element.5) | copy-start | bytes 4128772
  539.5 100.7 %copy-start.3 = (bf16[12,768]{1,0:T(8,128)(2,1)S(1)}, bf16[12,768]{1,0:T(8,128)(2,1)}, u32[]{:S(2)}) copy-start(bf16[12,768]{1,0:T(8,128)(2,1)} %param.4) | copy-start | bytes 55300
  616.9 8.5 %collective-permute-start = (f32[16,768]{1,0:T(8,128)S(1)}, f32[16,768]{1,0:T(8,128)S(1)}, u32[]{:S(2)}, u32[]{:S(2)}) collective-permute-start(f32[16,768]{1,0:T(8,128)S(1)} %fusion), channel_id=1, source_target_pairs={{0,1},{1,2},{2,3},{3,4},{4,5},{5,6},{6,7},{7,8},{8,9},{9,10},{10,1... | collective-permute-start | bytes 147464
  618.8 15.9 %collective-permute-start.1 = (f32[16,768]{1,0:T(8,128)S(1)}, f32[16,768]{1,0:T(8,128)S(1)}, u32[]{:S(2)}, u32[]{:S(2)}) collective-permute-start(f32[16,768]{1,0:T(8,128)S(1)} %fusion), channel_id=1, source_target_pairs={{0,2},{1,3},{2,4},{3,5},{4,6},{5,7},{6,8},{7,9},{8,10},{9,11},{10,... | collective-permute-start | bytes 147464
  620.2 3.9 collective-permute-start.7
  621.5 17.7 %collective-permute-start.2 = (f32[16,768]{1,0:T(8,128)S(1)}, f32[16,768]{1,0:T(8,128)S(1)}, u32[]{:S(2)}, u32[]{:S(2)}) collective-permute-start(f32[16,768]{1,0:T(8,128)S(1)} %fusion), channel_id=1, source_target_pairs={{0,3},{1,4},{2,5},{3,6},{4,7},{5,8},{6,9},{7,10},{8,11},{9,12},{10... | collective-permute-start | bytes 147464
  622.8 16.4 %collective-permute-start.3 = (f32[16,768]{1,0:T(8,128)S(1)}, f32[16,768]{1,0:T(8,128)S(1)}, u32[]{:S(2)}, u32[]{:S(2)}) collective-permute-start(f32[16,768]{1,0:T(8,128)S(1)} %fusion), channel_id=1, source_target_pairs={{0,4},{1,5},{2,6},{3,7},{4,8},{5,9},{6,10},{7,11},{8,12},{9,13},{1... | collective-permute-start | bytes 147464
  624.1 15.1 %collective-permute-start.4 = (f32[16,768]{1,0:T(8,128)S(1)}, f32[16,768]{1,0:T(8,128)S(1)}, u32[]{:S(2)}, u32[]{:S(2)}) collective-permute-start(f32[16,768]{1,0:T(8,128)S(1)} %fusion), channel_id=1, source_target_pairs={{0,5},{1,6},{2,7},{3,8},{4,9},{5,10},{6,11},{7,12},{8,13},{9,14},{... | collective-permute-start | bytes 147464
  625.4 13.8 %collective-permute-start.5 = (f32[16,768]{1,0:T(8,128)S(1)}, f32[16,768]{1,0:T(8,128)S(1)}, u32[]{:S(2)}, u32[]{:S(2)}) collective-permute-start(f32[16,768]{1,0:T(8,128)S(1)} %fusion), channel_id=1, source_target_pairs={{0,6},{1,7},{2,8},{3,9},{4,10},{5,11},{6,12},{7,13},{8,14},{9,15},... | collective-permute-start | bytes 147464
  634.7 4.5 collective-permute-start.6
Sparse Core Ops, SparseCore 0:
  166.9 294.6 all-reduce.4
where the time goes:
time: 652 us; the launch traced here: 648 us
  blocking collectives  301 us (46%)
  waiting for transfers between devices  295 us (45%)
  starting transfers between devices  20.2 us (3%)
  between operations  15.5 us (2%)
  matrix products  7.57 us (1%)
    psum x1, waiting for transfers between devices, on_device(): gate, up = lax.psum((gate_part, up_part), 'width')  295 us
    pmax x1, blocking collectives, on_device(): peak_in = lax.pmax(jnp.max(jnp.abs(inputs)), ('width', 'hidden'))  111 us
    unnamed x1, blocking collectives  77.4 us
    pmax x1, blocking collectives, on_device(): peak_act = lax.pmax(jnp.max(jnp.abs(act)), 'hidden')  70.6 us
    all_gather x1, blocking collectives, on_device(): gathered = lax.all_gather(source, 'hidden', axis=0, tiled=True)  42.5 us
    unnamed x8, starting transfers between devices  20.2 us
  transfers between devices with their start and end apart: 9, of which 1 were waited for; matrix products, arithmetic and copies ran while one was open for 0% of the time, Pallas kernels for 0%

commit v1 on v0

v1 whole, which is shorter than its diff:
```python
import jax
import jax.numpy as jnp
from jax import lax
from jax.experimental import pallas as pl
from jax.experimental.pallas import tpu as pltpu
from jax.sharding import PartitionSpec as P

F32 = jnp.float32
BF16 = jnp.bfloat16

PIECES = ((0, 2), (2, 2), (4, 2), (6, 1))
MAX_COPIES = 192


def ring_add(offset, value):
    return lax.rem(value + offset, 4)


def fold_max(values):
    rows, columns = values.shape
    total = None
    for row in range(0, rows, 8):
        for column in range(0, columns, 128):
            tile = jnp.abs(values[row : row + 8, column : column + 128])
            total = tile if total is None else jnp.maximum(total, tile)
    return total


def levels(tile, factor):
    peak = jnp.max(jnp.max(tile, axis=1, keepdims=True), axis=0, keepdims=True)
    level = 0.5 * (factor * peak + 1e-06)
    return level, 1.0 / level


def kernel(
    tokens, gate_hbm, up_hbm, down_hbm, out,
    gate_w, up_w, down_w, token_pad, token_z, token_f, token_x, scaled,
    keep, y_send, y_recv, z_sum, z_sum1, z_send, z_recv, act, act1, scaled_act,
    down_part, core_send, core_recv, x_send, x_recv, l_own, l_send, l_recv,
    peak_send, peak_recv, send_sem, recv_sem, load_sem,
):
    width, hidden = lax.axis_index("width"), lax.axis_index("hidden")
    y, zh = lax.div(width, 4), lax.rem(width, 4)
    core = lax.rem(hidden, 2)
    x, zl = lax.div(hidden, 8), lax.rem(lax.div(hidden, 2), 4)
    other = 1 - core

    def device(y_=None, zh_=None, x_=None, zl_=None, core_=None):
        y_ = y if y_ is None else y_
        zh_ = zh if zh_ is None else zh_
        x_ = x if x_ is None else x_
        zl_ = zl if zl_ is None else zl_
        core_ = core if core_ is None else core_
        return (y_ * 4 + zh_, (x_ * 4 + zl_) * 2 + core_)

    def along(axis, offset):
        if axis == "y":
            return device(y_=ring_add(offset, y))
        if axis == "zh":
            return device(zh_=ring_add(offset, zh))
        if axis == "x":
            return device(x_=ring_add(offset, x))
        if axis == "zl":
            return device(zl_=ring_add(offset, zl))
        return device(core_=other)

    copies = []

    def send(source, target, to):
        at = len(copies)
        copy = pltpu.make_async_remote_copy(
            src_ref=source, dst_ref=target,
            send_sem=send_sem.at[at], recv_sem=recv_sem.at[at],
            device_id=to, device_id_type=pl.DeviceIdType.MESH,
        )
        copies.append(copy)
        copy.start()
        return copy

    loads = []
    for at, (source, target) in enumerate(
        ((gate_hbm, gate_w), (up_hbm, up_w), (down_hbm, down_w))
    ):
        load = pltpu.make_async_copy(source, target, load_sem.at[at])
        load.start()
        loads.append(load)

    partners = [along(axis, offset) for axis in ("y", "zh", "x", "zl") for offset in (1, 2, 3)]
    partners.append(along("core", 1))
    barrier = pltpu.get_barrier_semaphore()
    for partner in partners:
        pl.semaphore_signal(barrier, inc=1, device_id=partner, device_id_type=pl.DeviceIdType.MESH)
    pl.semaphore_wait(barrier, len(partners))

    def peak_start(stage, axis, tile):
        peak_send[stage] = tile
        offsets = (1,) if axis == "core" else (1, 2, 3)
        return [
            send(peak_send.at[stage], peak_recv.at[stage, offset], along(axis, offset))
            for offset in offsets
        ]

    def peak_end(stage, sent, tile):
        for copy in sent:
            copy.wait_recv()
        for offset in range(1, len(sent) + 1):
            tile = jnp.maximum(tile, peak_recv[stage, offset])
        return tile

    token_pad[0:12, :] = tokens[...].astype(F32)
    token_pad[12:16, :] = jnp.zeros((4, 768), F32)
    padded = token_pad[...]
    token_z[zl] = padded.astype(BF16)
    zl_sent = [send(token_z.at[zl], token_z.at[zl], along("zl", o)) for o in (1, 2, 3)]
    tile = fold_max(padded)
    peak_sent = peak_start(0, "y", tile)
    tile = peak_end(0, peak_sent, tile)
    peak_sent = peak_start(1, "zh", tile)
    for copy in zl_sent:
        copy.wait_recv()
    for i in range(4):
        token_f[12 * i : 12 * i + 12, :] = token_z[i].astype(F32)[0:12, :]
    token_x[x, core] = token_f[...].astype(BF16)
    mine = token_x.at[x, core]
    to_right = send(mine, mine, along("x", 1))
    to_left = send(mine, mine, along("x", 3))
    core_sent = [send(mine, mine, along("core", 1))]
    tile = peak_end(1, peak_sent, tile)
    peak_sent = peak_start(2, "zl", tile)
    tile = peak_end(2, peak_sent, tile)
    peak_sent = peak_start(3, "core", tile)
    to_right.wait_recv()
    block = token_x.at[ring_add(3, x), core]
    part = block.at[:, 0:384]
    far = [send(part, part, along("x", 1))]
    core_sent.append(send(block, block, along("core", 1)))
    to_left.wait_recv()
    block = token_x.at[ring_add(1, x), core]
    part = block.at[:, 384:768]
    far.append(send(part, part, along("x", 3)))
    core_sent.append(send(block, block, along("core", 1)))
    tile = peak_end(3, peak_sent, tile)
    peak_sent = peak_start(4, "x", tile)
    for copy in far:
        copy.wait_recv()
    block = token_x.at[ring_add(2, x), core]
    core_sent.append(send(block, block, along("core", 1)))
    tile = peak_end(4, peak_sent, tile)
    level, inverse = levels(tile, 1.0)
    for copy in core_sent:
        copy.wait_recv()
    for j in range(4):
        for c in range(2):
            values = token_x[ring_add(j, y), c].astype(F32)
            row = 96 * j + 48 * c
            scaled[row : row + 48, :] = (level * jnp.tanh(values * inverse)).astype(BF16)

    loads[0].wait()
    loads[1].wait()

    state = [dict() for _ in PIECES]

    def ring_first(axis, sends, receives):
        ends = (along(axis, 1), along(axis, 3))
        return [send(sends(m), receives(m), ends[m % 2]) for m in range(4)]

    def ring_second(axis, m, sends, receives):
        return send(sends(m), receives(m), along(axis, 1 if m == 4 else 3))

    def quarter(k, q):
        if PIECES[k][1] == 2:
            return lax.rem(q, 2), pl.multiple_of(lax.div(q, 2) * 48, 48), 48
        return 0, pl.multiple_of(q * 32, 32), 32

    def multiply(k):
        first, count = PIECES[k]
        columns = slice(128 * first, 128 * (first + count))
        gate = jnp.dot(scaled[...], gate_w[:, columns], preferred_element_type=F32)
        for t in range(count):
            lanes = slice(128 * t, 128 * t + 128)
            y_send[0, first + t] = gate[192:288, lanes].astype(BF16)
            y_send[3, first + t] = gate[288:384, lanes].astype(BF16)
            keep[0, first + t] = gate[0:96, lanes]
            keep[1, first + t] = gate[96:192, lanes]
        up = jnp.dot(scaled[...], up_w[:, columns], preferred_element_type=F32)
        for t in range(count):
            lanes = slice(128 * t, 128 * t + 128)
            y_send[1, first + t] = up[192:288, lanes].astype(BF16)
            y_send[2, first + t] = up[96:192, lanes].astype(BF16)
            keep[2, first + t] = up[0:96, lanes]
            keep[3, first + t] = up[288:384, lanes]
        state[k]["y"] = ring_first(
            "y",
            lambda m: y_send.at[m, pl.ds(first, count)],
            lambda m: y_recv.at[m, pl.ds(first, count)],
        )

    def y_second(k):
        first, count = PIECES[k]
        for m, source, own in ((4, 0, 1), (5, 1, 3)):
            state[k]["y"][source].wait_recv()
            for t in range(first, first + count):
                y_send[m, t] = (keep[own, t] + y_recv[source, t].astype(F32)).astype(BF16)
            state[k]["y"].append(
                ring_second(
                    "y", m,
                    lambda m: y_send.at[m, pl.ds(first, count)],
                    lambda m: y_recv.at[m, pl.ds(first, count)],
                )
            )

    def z_read(k, g, q):
        tile_at, row, rows = quarter(k, q)
        if PIECES[k][1] == 2:
            return z_sum[k, g, tile_at, pl.ds(row, rows), :]
        return z_sum1[g, pl.ds(row, rows), :]

    def z_ref(ref, k, m):
        return ref.at[k, m, pl.ds(0, quarter(k, 0)[2])]

    def z_rows(k):
        return quarter(k, 0)[2]

    def y_third(k):
        first, count = PIECES[k]
        for m in (2, 3, 4, 5):
            state[k]["y"][m].wait_recv()
        for t in range(count):
            for g, own, one, two in ((0, 0, 3, 4), (1, 2, 2, 5)):
                total = (
                    keep[own, first + t]
                    + y_recv[one, first + t].astype(F32)
                    + y_recv[two, first + t].astype(F32)
                )
                if count == 2:
                    z_sum[k, g, t] = total
                else:
                    z_sum1[g, 0:96, :] = total
        if count == 1:
            z_sum1[:, 96:128, :] = jnp.zeros((2, 32, 128), F32)
        for m, g, j in ((0, 0, 2), (1, 1, 2), (2, 1, 1), (3, 0, 3)):
            z_send[k, m, 0 : z_rows(k), :] = z_read(k, g, ring_add(j, zh)).astype(BF16)
        state[k]["z"] = ring_first(
            "zh", lambda m: z_ref(z_send, k, m), lambda m: z_ref(z_recv, k, m)
        )

    def z_second(k):
        rows = z_rows(k)
        for m, source, g, j in ((4, 0, 0, 1), (5, 1, 1, 3)):
            state[k]["z"][source].wait_recv()
            own = z_read(k, g, ring_add(j, zh))
            z_send[k, m, 0:rows, :] = (own + z_recv[k, source, 0:rows, :].astype(F32)).astype(BF16)
            state[k]["z"].append(
                ring_second(
                    "zh", m, lambda m: z_ref(z_send, k, m), lambda m: z_ref(z_recv, k, m)
                )
            )

    def act_ref(k, owner_y, q, low, high):
        tile_at, row, _ = quarter(k, q)
        if PIECES[k][1] == 2:
            start = pl.multiple_of(owner_y * 96 + row + low, 16)
            return act.at[PIECES[k][0] + tile_at, pl.ds(start, high - low), :]
        return act1.at[owner_y, pl.ds(pl.multiple_of(row + low, 16), high - low), :]

    peaks = []

    def z_third(k):
        rows = z_rows(k)
        for m in (2, 3, 4, 5):
            state[k]["z"][m].wait_recv()
        gate, up = (
            z_read(k, g, zh)
            + z_recv[k, one, 0:rows, :].astype(F32)
            + z_recv[k, two, 0:rows, :].astype(F32)
            for g, one, two in ((0, 3, 4), (1, 2, 5))
        )
        value = gate / (1.0 + jnp.exp(-gate)) * up
        peaks.append(fold_max(value))
        mine = act_ref(k, y, zh, 0, rows)
        mine[...] = value.astype(BF16)
        state[k]["az"] = [send(mine, mine, along("zh", 1)), send(mine, mine, along("zh", 3))]

    def act_z_second(k):
        rows = z_rows(k)
        cut = 16 if rows == 32 or k % 2 else 32
        state[k]["az"][0].wait_recv()
        part = act_ref(k, y, ring_add(3, zh), 0, cut)
        far = [send(part, part, along("zh", 1))]
        state[k]["az"][1].wait_recv()
        part = act_ref(k, y, ring_add(1, zh), cut, rows)
        far.append(send(part, part, along("zh", 3)))
        state[k]["far"] = far

    def act_rows(k, owner_y, half=None):
        first, count = PIECES[k]
        if count == 2:
            rows = pl.ds(pl.multiple_of(owner_y * 96, 96), 96)
            if half is None:
                return act.at[pl.ds(first, 2), rows, :]
            return act.at[first + half, rows, :]
        if half is None:
            return act1.at[owner_y, pl.ds(0, 96), :]
        return act1.at[owner_y, pl.ds(48 * half, 48), :]

    def act_z_third(k):
        for copy in state[k]["far"]:
            copy.wait_recv()
        mine = act_rows(k, y)
        state[k]["ay"] = [send(mine, mine, along("y", 1)), send(mine, mine, along("y", 3))]

    def act_y_second(k):
        state[k]["ay"][0].wait_recv()
        part = act_rows(k, ring_add(3, y), 0)
        far = [send(part, part, along("y", 1))]
        state[k]["ay"][1].wait_recv()
        part = act_rows(k, ring_add(1, y), 1)
        far.append(send(part, part, along("y", 3)))
        state[k]["far"] = far

    def act_y_third(k):
        for copy in state[k]["far"]:
            copy.wait_recv()

    steps = (
        multiply, y_second, y_third, z_second, z_third,
        act_z_second, act_z_third, act_y_second, act_y_third,
    )
    order = ("core", "zl", "x", "zh", "y")
    last = len(PIECES) - 1
    peak_tile, peak_sent, stage = None, None, 0
    for time in range(len(steps) + last):
        for at in range(len(steps)):
            k = time - at
            if 0 <= k <= last:
                steps[at](k)
        if time >= last + 4 and stage < len(order):
            if stage == 0:
                peak_tile = peaks[0]
                for tile in peaks[1:]:
                    peak_tile = jnp.maximum(peak_tile, tile)
            else:
                peak_tile = peak_end(4 + stage, peak_sent, peak_tile)
            peak_sent = peak_start(5 + stage, order[stage], peak_tile)
            stage += 1
    peak_tile = peak_end(9, peak_sent, peak_tile)
    level, inverse = levels(peak_tile, 0.125)

    def saturated(values):
        return (level * jnp.tanh(values.astype(F32) * inverse)).astype(BF16)

    for t in range(6):
        scaled_act[:, 128 * t : 128 * t + 128] = saturated(act[t])
    for d in range(4):
        scaled_act[96 * d : 96 * d + 96, 768:896] = saturated(act1[d, 0:96, :])

    loads[2].wait()

    downs = [dict() for _ in range(3)]

    def down_multiply(n):
        result = jnp.dot(
            scaled_act[...], down_w[:, 256 * n : 256 * n + 256], preferred_element_type=F32
        )
        for half in range(2):
            for d in range(4):
                for c in range(2):
                    row = 96 * d + 48 * c
                    down_part[n, half, c, d] = result[row : row + 48, 128 * half : 128 * half + 128]
        core_send[n] = down_part[n, :, other].astype(BF16)
        downs[n]["core"] = send(core_send.at[n], core_recv.at[n], along("core", 1))

    def down_read(n, half, j):
        d = ring_add(j, x)
        return down_part[n, half, core, d] + core_recv[n, half, d].astype(F32)

    def down_x_first(n):
        downs[n]["core"].wait_recv()
        for m, half, j in ((0, 0, 2), (1, 1, 2), (2, 1, 1), (3, 0, 3)):
            x_send[n, m] = down_read(n, half, j).astype(BF16)
        downs[n]["x"] = ring_first("x", lambda m: x_send.at[n, m], lambda m: x_recv.at[n, m])

    def down_x_second(n):
        for m, source, half, j in ((4, 0, 0, 1), (5, 1, 1, 3)):
            downs[n]["x"][source].wait_recv()
            x_send[n, m] = (down_read(n, half, j) + x_recv[n, source].astype(F32)).astype(BF16)
            downs[n]["x"].append(
                ring_second("x", m, lambda m: x_send.at[n, m], lambda m: x_recv.at[n, m])
            )

    def down_x_third(n):
        for m in (2, 3, 4, 5):
            downs[n]["x"][m].wait_recv()
        for half, one, two in ((0, 3, 4), (1, 2, 5)):
            total = (
                down_read(n, half, 0)
                + x_recv[n, one].astype(F32)
                + x_recv[n, two].astype(F32)
            )
            for i in range(4):
                rows = total if i == 0 else pltpu.roll(total, 48 - 12 * i, 0)
                l_own[n, i, half] = rows[0:16, :]
                l_send[n, i, half] = rows[0:16, :].astype(BF16)
        downs[n]["l"] = [
            send(l_send.at[n, ring_add(o, zl)], l_recv.at[n, o], along("zl", o)) for o in (1, 2, 3)
        ]

    def down_last(n):
        for copy in downs[n]["l"]:
            copy.wait_recv()
        for half in range(2):
            total = l_own[n, zl, half]
            for o in (1, 2, 3):
                total = total + l_recv[n, o, half].astype(F32)
            lanes = slice(256 * n + 128 * half, 256 * n + 128 * half + 128)
            out[:, lanes] = (token_pad[0:12, lanes] + total[0:12, :]).astype(BF16)

    down_steps = (down_multiply, down_x_first, down_x_second, down_x_third, down_last)
    for time in range(len(down_steps) + 2):
        for at in range(len(down_steps)):
            n = time - at
            if 0 <= n < 3:
                down_steps[at](n)

    for copy in copies:
        copy.wait_send()


def on_device(tokens, gate_weight, up_weight, down_weight):
    vmem = pltpu.VMEM
    return pl.pallas_call(
        kernel,
        out_shape=jax.ShapeDtypeStruct((12, 768), BF16),
        in_specs=[pl.BlockSpec(memory_space=pltpu.VMEM)]
        + [pl.BlockSpec(memory_space=pl.ANY)] * 3,
        out_specs=pl.BlockSpec(memory_space=pltpu.VMEM),
        scratch_shapes=[
            vmem((768, 896), BF16),
            vmem((768, 896), BF16),
            vmem((896, 768), BF16),
            vmem((16, 768), F32),
            vmem((4, 16, 768), BF16),
            vmem((48, 768), F32),
            vmem((4, 2, 48, 768), BF16),
            vmem((384, 768), BF16),
            vmem((4, 7, 96, 128), F32),
            vmem((6, 7, 96, 128), BF16),
            vmem((6, 7, 96, 128), BF16),
            vmem((3, 2, 2, 96, 128), F32),
            vmem((2, 128, 128), F32),
            vmem((4, 6, 48, 128), BF16),
            vmem((4, 6, 48, 128), BF16),
            vmem((6, 384, 128), BF16),
            vmem((4, 128, 128), BF16),
            vmem((384, 896), BF16),
            vmem((3, 2, 2, 4, 48, 128), F32),
            vmem((3, 2, 4, 48, 128), BF16),
            vmem((3, 2, 4, 48, 128), BF16),
            vmem((3, 6, 48, 128), BF16),
            vmem((3, 6, 48, 128), BF16),
            vmem((3, 4, 2, 16, 128), F32),
            vmem((3, 4, 2, 16, 128), BF16),
            vmem((3, 4, 2, 16, 128), BF16),
            vmem((10, 8, 128), F32),
            vmem((10, 4, 8, 128), F32),
            pltpu.SemaphoreType.DMA((MAX_COPIES,)),
            pltpu.SemaphoreType.DMA((MAX_COPIES,)),
            pltpu.SemaphoreType.DMA((3,)),
        ],
        compiler_params=pltpu.CompilerParams(
            collective_id=0, has_side_effects=True, vmem_limit_bytes=40 * 1024 * 1024
        ),
        cost_estimate=pl.CostEstimate(
            flops=6 * 384 * 768 * 896, bytes_accessed=3 * 2 * 768 * 896, transcendentals=1000000
        ),
        name="swiglu_block",
    )(tokens, gate_weight, up_weight, down_weight)


def solution(mesh):
    in_specs = (
        P("hidden", "width"),
        P("width", "hidden"),
        P("width", "hidden"),
        P("hidden", "width"),
    )
    return jax.shard_map(
        on_device, mesh=mesh, in_specs=in_specs, out_specs=P("hidden", "width"), check_vma=False
    )
```

time: 652 us -> 116 us (0.18)
  blocking collectives: 301 us -> 0 us
  waiting for transfers between devices: 295 us -> 0 us
  Pallas kernels: 0 us -> 109 us
  starting transfers between devices: 20.2 us -> 0 us
  between operations: 15.5 us -> 0.01 us
  matrix products: 7.57 us -> 0 us
    psum x1 -> x0, waiting for transfers between devices: 295 us -> none  [on_device(): gate, up = lax.psum((gate_part, up_part), 'width')]
    pmax x2 -> x0, blocking collectives: 182 us -> none  [the longest x1 111 us: on_device(): peak_in = lax.pmax(jnp.max(jnp.abs(inputs)), ('width', 'hidden'))]
    pallas_call x0 -> x1, Pallas kernels: none -> 109 us  [on_device(): pl.pallas_call(kernel, out_shape=jax.ShapeDtypeStruct((12, 768), BF16), i...]
    unnamed x1 -> x0, blocking collectives: 77.4 us -> none
    all_gather x1 -> x0, blocking collectives: 42.5 us -> none  [on_device(): gathered = lax.all_gather(source, 'hidden', axis=0, tiled=True)]
    unnamed x8 -> x0, starting transfers between devices: 20.2 us -> none
    dot_general x3 -> x0, matrix products: 7.57 us -> none  [the longest x1 3.87 us: on_device(): jnp.dot(scaled_act, down_weight, preferred_element_type=jnp.float32)]
  transfers between devices with their start and end apart: 9 -> 0, of which waited for: 1 -> 0; matrix products, arithmetic and copies ran while one was open for 0% -> 0% of each run, Pallas kernels for 0% -> 0%
where the time goes in v1:
time: 116 us; the launch traced here: 115 us
  Pallas kernels  109 us (94%)
  local copies, waits for them, and re-layouts  5.36 us (5%)
    pallas_call x1, Pallas kernels, on_device(): pl.pallas_call(kernel, out_shape=jax.ShapeDtypeStruct((12, 768), BF16), i...  109 us
    unnamed x9, local copies, waits for them, and re-layouts  5.36 us

profile of v1, /device:TPU:1, one launch (start us, length us, event | category | flops | bytes accessed | tf_op | source)
XLA Modules:
  0.0 114.8 jit_solution(24982481440304569)
XLA Ops:
  0.0 0.0 copy-start
  0.0 1.3 %copy-done = bf16[768,896]{1,0:T(8,128)(2,1)S(1)} copy-done((bf16[768,896]{1,0:T(8,128)(2,1)S(1)}, bf16[768,896]{1,0:T(8,128)(2,1)}, u32[]{:S(2)}) %copy-start) | copy-done | bytes 1376280
  1.3 0.0 copy-start.1
  1.3 1.3 %copy-done.1 = bf16[768,896]{1,0:T(8,128)(2,1)S(1)} copy-done((bf16[768,896]{1,0:T(8,128)(2,1)S(1)}, bf16[768,896]{1,0:T(8,128)(2,1)}, u32[]{:S(2)}) %copy-start.1) | copy-done | bytes 1376280
  2.7 0.0 copy-start.2
  2.7 1.3 %copy-done.2 = bf16[896,768]{1,0:T(8,128)(2,1)S(1)} copy-done((bf16[896,768]{1,0:T(8,128)(2,1)S(1)}, bf16[896,768]{1,0:T(8,128)(2,1)}, u32[]{:S(2)}) %copy-start.2) | copy-done | bytes 1376280
  4.0 0.0 copy-start.3
  4.0 0.7 copy-done.3
  4.8 109.5 %swiglu_block.1 = bf16[12,768]{1,0:T(8,128)(2,1)S(1)} custom-call(bf16[12,768]{1,0:T(8,128)(2,1)S(1)} %copy-done.3, bf16[768,896]{1,0:T(8,128)(2,1)S(1)} %copy-done, bf16[768,896]{1,0:T(8,128)(2,1)S(1)} %copy-done.1, bf16[896,768]{1,0:T(8,128)(2,1)S(1)} %copy-done.2), custom_call_target="tpu_custom_call" | custom-call | flops 1585446912 | bytes 4128768 | tf_op jit(solution)/shard_map/swiglu_block/pallas_call | solution.py:431
  114.2 0.6 copy.6
Async XLA Ops:
  0.0 1.3 %copy-start = (bf16[768,896]{1,0:T(8,128)(2,1)S(1)}, bf16[768,896]{1,0:T(8,128)(2,1)}, u32[]{:S(2)}) copy-start(bf16[768,896]{1,0:T(8,128)(2,1)} %gate_hbm.1) | copy-start | bytes 4128772
  1.3 1.3 %copy-start.1 = (bf16[768,896]{1,0:T(8,128)(2,1)S(1)}, bf16[768,896]{1,0:T(8,128)(2,1)}, u32[]{:S(2)}) copy-start(bf16[768,896]{1,0:T(8,128)(2,1)} %up_hbm.1) | copy-start | bytes 4128772
  2.7 1.3 %copy-start.2 = (bf16[896,768]{1,0:T(8,128)(2,1)S(1)}, bf16[896,768]{1,0:T(8,128)(2,1)}, u32[]{:S(2)}) copy-start(bf16[896,768]{1,0:T(8,128)(2,1)} %down_hbm.1) | copy-start | bytes 4128772
  4.0 0.7 copy-start.3

commit v2 on v1

v2 whole, which is shorter than its diff:
```python
import jax
import jax.numpy as jnp
from jax import lax
from jax.experimental import pallas as pl
from jax.experimental.pallas import tpu as pltpu
from jax.sharding import PartitionSpec as P

F32 = jnp.float32
BF16 = jnp.bfloat16

PIECES = ((0, 2), (2, 2), (4, 2), (6, 1))
MAX_COPIES = 256


def ring_add(offset, value):
    return lax.rem(value + offset, 4)


def fold_max(values):
    rows, columns = values.shape
    total = None
    for row in range(0, rows, 8):
        for column in range(0, columns, 128):
            tile = jnp.abs(values[row : row + 8, column : column + 128])
            total = tile if total is None else jnp.maximum(total, tile)
    return total


def levels(tile, factor):
    peak = jnp.max(jnp.max(tile, axis=1, keepdims=True), axis=0, keepdims=True)
    level = 0.5 * (factor * peak + 1e-06)
    return level, 1.0 / level


def kernel(
    tokens, gate_hbm, up_hbm, down_hbm, out,
    gate_w, up_w, down_w, token_in, token_pad, token_z, token_f, token_x, scaled,
    keep, y_send, y_recv, z_sum, z_sum1, z_send, z_recv, act, act1, scaled_act,
    down_part, core_send, core_recv, x_send, x_recv, l_own, l_send, l_recv,
    peak_send, peak_recv, send_sem, recv_sem, load_sem,
):
    width, hidden = lax.axis_index("width"), lax.axis_index("hidden")
    y, zh = lax.div(width, 4), lax.rem(width, 4)
    core = lax.rem(hidden, 2)
    x, zl = lax.div(hidden, 8), lax.rem(lax.div(hidden, 2), 4)
    other = 1 - core

    def device(y_=None, zh_=None, x_=None, zl_=None, core_=None):
        y_ = y if y_ is None else y_
        zh_ = zh if zh_ is None else zh_
        x_ = x if x_ is None else x_
        zl_ = zl if zl_ is None else zl_
        core_ = core if core_ is None else core_
        return (y_ * 4 + zh_, (x_ * 4 + zl_) * 2 + core_)

    def along(axis, offset):
        if axis == "y":
            return device(y_=ring_add(offset, y))
        if axis == "zh":
            return device(zh_=ring_add(offset, zh))
        if axis == "x":
            return device(x_=ring_add(offset, x))
        if axis == "zl":
            return device(zl_=ring_add(offset, zl))
        return device(core_=other)

    copies = []

    def send(source, target, to):
        at = len(copies)
        copy = pltpu.make_async_remote_copy(
            src_ref=source, dst_ref=target,
            send_sem=send_sem.at[at], recv_sem=recv_sem.at[at],
            device_id=to, device_id_type=pl.DeviceIdType.MESH,
        )
        copies.append(copy)
        copy.start()
        return copy

    loads = []
    for at, (source, target) in reversed(list(enumerate(
        ((gate_hbm, gate_w), (up_hbm, up_w), (down_hbm, down_w), (tokens, token_in))
    ))):
        load = pltpu.make_async_copy(source, target, load_sem.at[at])
        load.start()
        loads.insert(0, load)

    def z_partner(offset):
        z = lax.rem(zh * 4 + zl + offset, 16)
        return device(zh_=lax.div(z, 4), zl_=lax.rem(z, 4))

    def plane_partner(offset):
        return device(x_=ring_add(offset // 4, x), y_=ring_add(offset % 4, y))

    groups = (
        [along("core", 1)],
        [z_partner(o) for o in range(1, 16)],
        [plane_partner(o) for o in range(1, 16)],
    )
    partners = [partner for group in groups for partner in group]
    barrier = pltpu.get_barrier_semaphore()
    for partner in partners:
        pl.semaphore_signal(barrier, inc=1, device_id=partner, device_id_type=pl.DeviceIdType.MESH)
    pl.semaphore_wait(barrier, len(partners))

    def peak_start(use, stage, tile):
        at = 3 * use + stage
        peak_send[at] = tile
        return [
            send(peak_send.at[at], peak_recv.at[at, o], to) for o, to in enumerate(groups[stage])
        ]

    def peak_end(use, stage, sent, tile):
        for o, copy in enumerate(sent):
            copy.wait_recv()
            tile = jnp.maximum(tile, peak_recv[3 * use + stage, o])
        return tile

    loads[3].wait()
    token_pad[0:12, :] = token_in[...].astype(F32)
    token_pad[12:16, :] = jnp.zeros((4, 768), F32)
    padded = token_pad[...]
    token_z[zl] = padded.astype(BF16)
    tile = fold_max(padded)
    peak_sent = peak_start(0, 0, tile)
    zl_sent = [send(token_z.at[zl], token_z.at[zl], along("zl", o)) for o in (1, 2, 3)]
    tile = peak_end(0, 0, peak_sent, tile)
    peak_sent = peak_start(0, 1, tile)
    for copy in zl_sent:
        copy.wait_recv()
    for i in range(4):
        token_f[12 * i : 12 * i + 12, :] = token_z[i].astype(F32)[0:12, :]
    token_x[x, core] = token_f[...].astype(BF16)
    mine = token_x.at[x, core]
    core_sent = [send(mine, mine, along("core", 1))]
    x_sent = [send(mine, mine, along("x", o)) for o in (1, 3, 2)]
    for o in (0, 1):
        x_sent[o].wait_recv()
        block = token_x.at[ring_add((3, 1)[o], x), core]
        core_sent.append(send(block, block, along("core", 1)))
    tile = peak_end(0, 1, peak_sent, tile)
    peak_sent = peak_start(0, 2, tile)
    x_sent[2].wait_recv()
    block = token_x.at[ring_add(2, x), core]
    core_sent.append(send(block, block, along("core", 1)))
    for copy in core_sent:
        copy.wait_recv()
    tile = peak_end(0, 2, peak_sent, tile)
    level, inverse = levels(tile, 1.0)
    for j in range(4):
        for c in range(2):
            values = token_x[ring_add(j, y), c].astype(F32)
            row = 96 * j + 48 * c
            scaled[row : row + 48, :] = (level * jnp.tanh(values * inverse)).astype(BF16)

    loads[0].wait()
    loads[1].wait()

    state = [dict() for _ in PIECES]

    def ring_first(axis, sends, receives):
        ends = (along(axis, 1), along(axis, 3))
        return [send(sends(m), receives(m), ends[m % 2]) for m in range(4)]

    def ring_second(axis, m, sends, receives):
        return send(sends(m), receives(m), along(axis, 1 if m == 4 else 3))

    def quarter(k, q):
        if PIECES[k][1] == 2:
            return lax.rem(q, 2), pl.multiple_of(lax.div(q, 2) * 48, 48), 48
        return 0, pl.multiple_of(q * 32, 32), 32

    def multiply(k):
        first, count = PIECES[k]
        columns = slice(128 * first, 128 * (first + count))
        gate = jnp.dot(scaled[...], gate_w[:, columns], preferred_element_type=F32)
        for t in range(count):
            lanes = slice(128 * t, 128 * t + 128)
            y_send[0, first + t] = gate[192:288, lanes].astype(BF16)
            y_send[3, first + t] = gate[288:384, lanes].astype(BF16)
            keep[0, first + t] = gate[0:96, lanes]
            keep[1, first + t] = gate[96:192, lanes]
        up = jnp.dot(scaled[...], up_w[:, columns], preferred_element_type=F32)
        for t in range(count):
            lanes = slice(128 * t, 128 * t + 128)
            y_send[1, first + t] = up[192:288, lanes].astype(BF16)
            y_send[2, first + t] = up[96:192, lanes].astype(BF16)
            keep[2, first + t] = up[0:96, lanes]
            keep[3, first + t] = up[288:384, lanes]
        state[k]["y"] = ring_first(
            "y",
            lambda m: y_send.at[m, pl.ds(first, count)],
            lambda m: y_recv.at[m, pl.ds(first, count)],
        )

    def y_second(k):
        first, count = PIECES[k]
        for m, source, own in ((4, 0, 1), (5, 1, 3)):
            state[k]["y"][source].wait_recv()
            for t in range(first, first + count):
                y_send[m, t] = (keep[own, t] + y_recv[source, t].astype(F32)).astype(BF16)
            state[k]["y"].append(
                ring_second(
                    "y", m,
                    lambda m: y_send.at[m, pl.ds(first, count)],
                    lambda m: y_recv.at[m, pl.ds(first, count)],
                )
            )

    def z_read(k, g, q):
        tile_at, row, rows = quarter(k, q)
        if PIECES[k][1] == 2:
            return z_sum[k, g, tile_at, pl.ds(row, rows), :]
        return z_sum1[g, pl.ds(row, rows), :]

    def z_rows(k):
        return quarter(k, 0)[2]

    def y_third(k):
        first, count = PIECES[k]
        for m in (2, 3, 4, 5):
            state[k]["y"][m].wait_recv()
        for t in range(count):
            for g, own, one, two in ((0, 0, 3, 4), (1, 2, 2, 5)):
                total = (
                    keep[own, first + t]
                    + y_recv[one, first + t].astype(F32)
                    + y_recv[two, first + t].astype(F32)
                )
                if count == 2:
                    z_sum[k, g, t] = total
                else:
                    z_sum1[g, 0:96, :] = total
        if count == 1:
            z_sum1[:, 96:128, :] = jnp.zeros((2, 32, 128), F32)
        rows = z_rows(k)
        state[k]["z"] = []
        for o in (2, 1, 3):
            for g in range(2):
                z_send[k, o - 1, g, 0:rows, :] = z_read(k, g, ring_add(o, zh)).astype(BF16)
            state[k]["z"].append(
                send(
                    z_send.at[k, o - 1, :, pl.ds(0, rows)],
                    z_recv.at[k, o - 1, :, pl.ds(0, rows)],
                    along("zh", o),
                )
            )

    def act_ref(k, owner_y, q):
        tile_at, row, rows = quarter(k, q)
        if PIECES[k][1] == 2:
            start = pl.multiple_of(owner_y * 96 + row, 16)
            return act.at[PIECES[k][0] + tile_at, pl.ds(start, rows), :]
        return act1.at[owner_y, pl.ds(row, rows), :]

    peaks = []

    def z_third(k):
        rows = z_rows(k)
        for copy in state[k]["z"]:
            copy.wait_recv()
        gate, up = (
            z_read(k, g, zh) + sum(z_recv[k, o, g, 0:rows, :].astype(F32) for o in range(3))
            for g in range(2)
        )
        value = gate / (1.0 + jnp.exp(-gate)) * up
        peaks.append(fold_max(value))
        mine = act_ref(k, y, zh)
        mine[...] = value.astype(BF16)
        state[k]["az"] = [send(mine, mine, along("zh", o)) for o in (2, 1, 3)]

    def act_z_end(k):
        for copy in state[k]["az"]:
            copy.wait_recv()
        first, count = PIECES[k]
        if count == 2:
            mine = act.at[pl.ds(first, 2), pl.ds(pl.multiple_of(y * 96, 96), 96), :]
        else:
            mine = act1.at[y, pl.ds(0, 96), :]
        state[k]["ay"] = [send(mine, mine, along("y", o)) for o in (2, 1, 3)]

    def act_y_end(k):
        for copy in state[k]["ay"]:
            copy.wait_recv()

    def every(step, count=len(PIECES)):
        for k in range(count):
            step(k)

    for step, k in (
        (multiply, 0), (multiply, 1), (y_second, 0), (multiply, 2), (y_second, 1),
        (multiply, 3), (y_third, 0), (y_second, 2), (y_third, 1), (y_second, 3),
        (y_third, 2), (y_third, 3),
    ):
        step(k)
    every(z_third)
    tile = peaks[0]
    for more in peaks[1:]:
        tile = jnp.maximum(tile, more)
    peak_sent = peak_start(1, 0, tile)
    act_z_end(0)
    tile = peak_end(1, 0, peak_sent, tile)
    peak_sent = peak_start(1, 1, tile)
    for k in range(1, len(PIECES)):
        act_z_end(k)
    tile = peak_end(1, 1, peak_sent, tile)
    peak_sent = peak_start(1, 2, tile)
    every(act_y_end)
    tile = peak_end(1, 2, peak_sent, tile)
    level, inverse = levels(tile, 0.125)

    def saturated(values):
        return (level * jnp.tanh(values.astype(F32) * inverse)).astype(BF16)

    for t in range(6):
        scaled_act[:, 128 * t : 128 * t + 128] = saturated(act[t])
    for d in range(4):
        scaled_act[96 * d : 96 * d + 96, 768:896] = saturated(act1[d, 0:96, :])

    loads[2].wait()

    downs = [dict() for _ in range(3)]

    def down_multiply(n):
        result = jnp.dot(
            scaled_act[...], down_w[:, 256 * n : 256 * n + 256], preferred_element_type=F32
        )
        for half in range(2):
            for d in range(4):
                for c in range(2):
                    row = 96 * d + 48 * c
                    down_part[n, half, c, d] = result[row : row + 48, 128 * half : 128 * half + 128]
        core_send[n] = down_part[n, :, other].astype(BF16)
        downs[n]["core"] = send(core_send.at[n], core_recv.at[n], along("core", 1))

    def down_read(n, half, j):
        d = ring_add(j, x)
        return down_part[n, half, core, d] + core_recv[n, half, d].astype(F32)

    def down_x_first(n):
        downs[n]["core"].wait_recv()
        downs[n]["x"] = []
        for o in (2, 1, 3):
            for half in range(2):
                x_send[n, o - 1, half] = down_read(n, half, o).astype(BF16)
            downs[n]["x"].append(send(x_send.at[n, o - 1], x_recv.at[n, o - 1], along("x", o)))

    def down_l_first(n):
        for copy in downs[n]["x"]:
            copy.wait_recv()
        for half in range(2):
            total = down_read(n, half, 0) + sum(x_recv[n, o, half].astype(F32) for o in range(3))
            for i in range(4):
                rows = total if i == 0 else pltpu.roll(total, 48 - 12 * i, 0)
                l_own[n, i, half] = rows[0:16, :]
                l_send[n, i, half] = rows[0:16, :].astype(BF16)
        downs[n]["l"] = [
            send(l_send.at[n, ring_add(o, zl)], l_recv.at[n, o], along("zl", o)) for o in (1, 2, 3)
        ]

    def down_last(n):
        for copy in downs[n]["l"]:
            copy.wait_recv()
        for half in range(2):
            total = l_own[n, zl, half]
            for o in (1, 2, 3):
                total = total + l_recv[n, o, half].astype(F32)
            lanes = slice(256 * n + 128 * half, 256 * n + 128 * half + 128)
            out[:, lanes] = (token_pad[0:12, lanes] + total[0:12, :]).astype(BF16)

    for step in (down_multiply, down_x_first, down_l_first, down_last):
        every(step, 3)

    for copy in copies:
        copy.wait_send()


def on_device(tokens, gate_weight, up_weight, down_weight):
    vmem = pltpu.VMEM
    return pl.pallas_call(
        kernel,
        out_shape=jax.ShapeDtypeStruct((12, 768), BF16),
        in_specs=[pl.BlockSpec(memory_space=pl.ANY)] * 4,
        out_specs=pl.BlockSpec(memory_space=pltpu.VMEM),
        scratch_shapes=[
            vmem((768, 896), BF16),
            vmem((768, 896), BF16),
            vmem((896, 768), BF16),
            vmem((12, 768), BF16),
            vmem((16, 768), F32),
            vmem((4, 16, 768), BF16),
            vmem((48, 768), F32),
            vmem((4, 2, 48, 768), BF16),
            vmem((384, 768), BF16),
            vmem((4, 7, 96, 128), F32),
            vmem((6, 7, 96, 128), BF16),
            vmem((6, 7, 96, 128), BF16),
            vmem((3, 2, 2, 96, 128), F32),
            vmem((2, 128, 128), F32),
            vmem((4, 3, 2, 48, 128), BF16),
            vmem((4, 3, 2, 48, 128), BF16),
            vmem((6, 384, 128), BF16),
            vmem((4, 128, 128), BF16),
            vmem((384, 896), BF16),
            vmem((3, 2, 2, 4, 48, 128), F32),
            vmem((3, 2, 4, 48, 128), BF16),
            vmem((3, 2, 4, 48, 128), BF16),
            vmem((3, 3, 2, 48, 128), BF16),
            vmem((3, 3, 2, 48, 128), BF16),
            vmem((3, 4, 2, 16, 128), F32),
            vmem((3, 4, 2, 16, 128), BF16),
            vmem((3, 4, 2, 16, 128), BF16),
            vmem((6, 8, 128), F32),
            vmem((6, 15, 8, 128), F32),
            pltpu.SemaphoreType.DMA((MAX_COPIES,)),
            pltpu.SemaphoreType.DMA((MAX_COPIES,)),
            pltpu.SemaphoreType.DMA((4,)),
        ],
        compiler_params=pltpu.CompilerParams(
            collective_id=0, has_side_effects=True, vmem_limit_bytes=60 * 1024 * 1024
        ),
        cost_estimate=pl.CostEstimate(
            flops=6 * 384 * 768 * 896, bytes_accessed=3 * 2 * 768 * 896, transcendentals=1000000
        ),
        name="swiglu_block",
    )(tokens, gate_weight, up_weight, down_weight)


def solution(mesh):
    in_specs = (
        P("hidden", "width"),
        P("width", "hidden"),
        P("width", "hidden"),
        P("hidden", "width"),
    )
    return jax.shard_map(
        on_device, mesh=mesh, in_specs=in_specs, out_specs=P("hidden", "width"), check_vma=False
    )
```

time: 116 us -> 95.7 us (0.83)
  Pallas kernels: 109 us -> 94.1 us
  local copies, waits for them, and re-layouts: 5.36 us -> 1.35 us
    pallas_call x1, Pallas kernels: 109 us -> 94.1 us  [on_device(): pl.pallas_call(kernel, out_shape=jax.ShapeDtypeStruct((12, 768), BF16), i...]
    unnamed x9 -> x1, local copies, waits for them, and re-layouts: 5.36 us -> 1.35 us
where the time goes in v2:
time: 95.7 us; the launch traced here: 95.5 us
  Pallas kernels  94.1 us (98%)
  local copies, waits for them, and re-layouts  1.35 us (1%)
    pallas_call x1, Pallas kernels, on_device(): pl.pallas_call(kernel, out_shape=jax.ShapeDtypeStruct((12, 768), BF16), i...  94.1 us

profile of v2, /device:TPU:1, one launch (start us, length us, event | category | flops | bytes accessed | tf_op | source)
XLA Modules:
  0.0 95.5 jit_solution(2493370539588760572)
XLA Ops:
  0.0 94.1 %swiglu_block.1 = bf16[12,768]{1,0:T(8,128)(2,1)} custom-call(bf16[12,768]{1,0:T(8,128)(2,1)} %tokens.1, bf16[768,896]{1,0:T(8,128)(2,1)} %gate_hbm.1, bf16[768,896]{1,0:T(8,128)(2,1)} %up_hbm.1, bf16[896,768]{1,0:T(8,128)(2,1)} %down_hbm.1), custom_call_target="tpu_custom_call" | custom-call | flops 1585446912 | bytes 4128768 | tf_op jit(solution)/shard_map/swiglu_block/pallas_call | solution.py:380
  94.2 1.3 %copy.6 = bf16[12,768]{1,0:T(8,128)(2,1)} copy(bf16[12,768]{1,0:T(8,128)(2,1)} %swiglu_block.1) | data formatting | bytes 36864

commit v3 on v2

--- a/solution.py
+++ b/solution.py
@@ -8,7 +8,15 @@
 F32 = jnp.float32
 BF16 = jnp.bfloat16
 
-PIECES = ((0, 2), (2, 2), (4, 2), (6, 1))
+PIECES = ((6, 1), (0, 2), (2, 2), (4, 2))
+Y_RING = (False, True, True, True)
+Z_RING = (False, True, True, False)
+STEPS = [(name[0], int(name[1])) for name in (
+    "M0", "M1", "M2", "M3", "N1", "N2", "S1", "S2", "N3", "Y0",
+    "S3", "Y1", "Y2", "Y3", "A0", "Z1", "Z2", "A3", "A1", "A2",
+)]
+Z_ORDER = sorted(range(1, 16), key=lambda o: -min(o, 16 - o))
+PLANE_ORDER = sorted(range(1, 16), key=lambda o: abs(o // 4 - 2) + abs(o % 4 - 2))
 MAX_COPIES = 256
 
 
@@ -23,11 +31,11 @@
         for column in range(0, columns, 128):
             tile = jnp.abs(values[row : row + 8, column : column + 128])
             total = tile if total is None else jnp.maximum(total, tile)
-    return total
+    return jnp.max(total, axis=0, keepdims=True)
 
 
 def levels(tile, factor):
-    peak = jnp.max(jnp.max(tile, axis=1, keepdims=True), axis=0, keepdims=True)
+    peak = jnp.max(tile, axis=1, keepdims=True)
     level = 0.5 * (factor * peak + 1e-06)
     return level, 1.0 / level
 
@@ -94,10 +102,10 @@
 
     groups = (
         [along("core", 1)],
-        [z_partner(o) for o in range(1, 16)],
-        [plane_partner(o) for o in range(1, 16)],
+        [z_partner(o) for o in Z_ORDER],
+        [plane_partner(o) for o in PLANE_ORDER],
     )
-    partners = [partner for group in groups for partner in group]
+    partners = groups[1] + groups[2] + groups[0]
     barrier = pltpu.get_barrier_semaphore()
     for partner in partners:
         pl.semaphore_signal(barrier, inc=1, device_id=partner, device_id_type=pl.DeviceIdType.MESH)
@@ -158,40 +166,58 @@
 
     state = [dict() for _ in PIECES]
 
-    def ring_first(axis, sends, receives):
+    def ring_sends(axis, which, sends, receives):
         ends = (along(axis, 1), along(axis, 3))
-        return [send(sends(m), receives(m), ends[m % 2]) for m in range(4)]
-
-    def ring_second(axis, m, sends, receives):
-        return send(sends(m), receives(m), along(axis, 1 if m == 4 else 3))
+        return {m: send(sends(m), receives(m), ends[m % 2]) for m in which}
 
     def quarter(k, q):
         if PIECES[k][1] == 2:
             return lax.rem(q, 2), pl.multiple_of(lax.div(q, 2) * 48, 48), 48
         return 0, pl.multiple_of(q * 32, 32), 32
 
+    def y_ring(k, which):
+        tiles = pl.ds(*PIECES[k])
+        return ring_sends("y", which, lambda m: y_send.at[m, tiles], lambda m: y_recv.at[m, tiles])
+
+    def y_near(k):
+        state[k]["y"].update(y_ring(k, (2, 3)))
+
+    def z_ring(k, which):
+        return ring_sends("zh", which, lambda m: z_slot(z_send, k, m), lambda m: z_slot(z_recv, k, m))
+
     def multiply(k):
         first, count = PIECES[k]
         columns = slice(128 * first, 128 * (first + count))
         gate = jnp.dot(scaled[...], gate_w[:, columns], preferred_element_type=F32)
+        up = jnp.dot(scaled[...], up_w[:, columns], preferred_element_type=F32)
+        tiles = pl.ds(first, count)
         for t in range(count):
             lanes = slice(128 * t, 128 * t + 128)
-            y_send[0, first + t] = gate[192:288, lanes].astype(BF16)
-            y_send[3, first + t] = gate[288:384, lanes].astype(BF16)
+            if Y_RING[k]:
+                y_send[0, first + t] = gate[192:288, lanes].astype(BF16)
+                y_send[1, first + t] = up[192:288, lanes].astype(BF16)
+                y_send[2, first + t] = up[96:192, lanes].astype(BF16)
+                y_send[3, first + t] = gate[288:384, lanes].astype(BF16)
+                keep[1, first + t] = gate[96:192, lanes]
+                keep[3, first + t] = up[288:384, lanes]
+            else:
+                for o in range(3):
+                    rows = slice(96 * o + 96, 96 * o + 192)
+                    y_send[2 * o, first + t] = gate[rows, lanes].astype(BF16)
+                    y_send[2 * o + 1, first + t] = up[rows, lanes].astype(BF16)
             keep[0, first + t] = gate[0:96, lanes]
-            keep[1, first + t] = gate[96:192, lanes]
-        up = jnp.dot(scaled[...], up_w[:, columns], preferred_element_type=F32)
-        for t in range(count):
-            lanes = slice(128 * t, 128 * t + 128)
-            y_send[1, first + t] = up[192:288, lanes].astype(BF16)
-            y_send[2, first + t] = up[96:192, lanes].astype(BF16)
             keep[2, first + t] = up[0:96, lanes]
-            keep[3, first + t] = up[288:384, lanes]
-        state[k]["y"] = ring_first(
-            "y",
-            lambda m: y_send.at[m, pl.ds(first, count)],
-            lambda m: y_recv.at[m, pl.ds(first, count)],
-        )
+        if Y_RING[k]:
+            state[k]["y"] = y_ring(k, (0, 1))
+        else:
+            state[k]["y"] = [
+                send(
+                    y_send.at[pl.ds(2 * o - 2, 2), tiles],
+                    y_recv.at[pl.ds(2 * o - 2, 2), tiles],
+                    along("y", o),
+                )
+                for o in (2, 1, 3)
+            ]
 
     def y_second(k):
         first, count = PIECES[k]
@@ -199,18 +225,12 @@
             state[k]["y"][source].wait_recv()
             for t in range(first, first + count):
                 y_send[m, t] = (keep[own, t] + y_recv[source, t].astype(F32)).astype(BF16)
-            state[k]["y"].append(
-                ring_second(
-                    "y", m,
-                    lambda m: y_send.at[m, pl.ds(first, count)],
-                    lambda m: y_recv.at[m, pl.ds(first, count)],
-                )
-            )
+            state[k]["y"].update(y_ring(k, (m,)))
 
     def z_read(k, g, q):
         tile_at, row, rows = quarter(k, q)
         if PIECES[k][1] == 2:
-            return z_sum[k, g, tile_at, pl.ds(row, rows), :]
+            return z_sum[PIECES[k][0] // 2, g, tile_at, pl.ds(row, rows), :]
         return z_sum1[g, pl.ds(row, rows), :]
 
     def z_rows(k):
@@ -218,22 +238,26 @@
 
     def y_third(k):
         first, count = PIECES[k]
-        for m in (2, 3, 4, 5):
+        ring = Y_RING[k]
+        for m in (2, 3, 4, 5) if ring else range(3):
             state[k]["y"][m].wait_recv()
         for t in range(count):
-            for g, own, one, two in ((0, 0, 3, 4), (1, 2, 2, 5)):
-                total = (
-                    keep[own, first + t]
-                    + y_recv[one, first + t].astype(F32)
-                    + y_recv[two, first + t].astype(F32)
-                )
+            for g, arrived in ((0, (3, 4) if ring else (0, 2, 4)), (1, (2, 5) if ring else (1, 3, 5))):
+                total = keep[2 * g, first + t]
+                for m in arrived:
+                    total = total + y_recv[m, first + t].astype(F32)
                 if count == 2:
-                    z_sum[k, g, t] = total
+                    z_sum[PIECES[k][0] // 2, g, t] = total
                 else:
                     z_sum1[g, 0:96, :] = total
         if count == 1:
             z_sum1[:, 96:128, :] = jnp.zeros((2, 32, 128), F32)
         rows = z_rows(k)
+        if Z_RING[k]:
+            for m, g, j in ((0, 0, 2), (1, 1, 2), (2, 1, 1), (3, 0, 3)):
+                z_send[k, m // 2, m % 2, 0:rows, :] = z_read(k, g, ring_add(j, zh)).astype(BF16)
+            state[k]["z"] = z_ring(k, range(4))
+            return
         state[k]["z"] = []
         for o in (2, 1, 3):
             for g in range(2):
@@ -246,6 +270,17 @@
                 )
             )
 
+    def z_slot(ref, k, m):
+        return ref.at[k, m // 2, m % 2, pl.ds(0, z_rows(k))]
+
+    def z_second(k):
+        rows = z_rows(k)
+        for m, g, j in ((4, 0, 1), (5, 1, 3)):
+            state[k]["z"][m - 4].wait_recv()
+            total = z_read(k, g, ring_add(j, zh)) + z_recv[k, 0, m - 4, 0:rows, :].astype(F32)
+            z_send[k, 2, m - 4, 0:rows, :] = total.astype(BF16)
+            state[k]["z"].update(z_ring(k, (m,)))
+
     def act_ref(k, owner_y, q):
         tile_at, row, rows = quarter(k, q)
         if PIECES[k][1] == 2:
@@ -257,12 +292,18 @@
 
     def z_third(k):
         rows = z_rows(k)
-        for copy in state[k]["z"]:
-            copy.wait_recv()
-        gate, up = (
-            z_read(k, g, zh) + sum(z_recv[k, o, g, 0:rows, :].astype(F32) for o in range(3))
-            for g in range(2)
-        )
+        ring = Z_RING[k]
+        for m in (2, 3, 4, 5) if ring else range(3):
+            state[k]["z"][m].wait_recv()
+
+        def summed(g, arrived):
+            total = z_read(k, g, zh)
+            for m in arrived:
+                total = total + z_recv[k, m // 2, m % 2, 0:rows, :].astype(F32)
+            return total
+
+        gate = summed(0, (3, 4) if ring else (0, 2, 4))
+        up = summed(1, (2, 5) if ring else (1, 3, 5))
         value = gate / (1.0 + jnp.exp(-gate)) * up
         peaks.append(fold_max(value))
         mine = act_ref(k, y, zh)
@@ -287,26 +328,22 @@
         for k in range(count):
             step(k)
 
-    for step, k in (
-        (multiply, 0), (multiply, 1), (y_second, 0), (multiply, 2), (y_second, 1),
-        (multiply, 3), (y_third, 0), (y_second, 2), (y_third, 1), (y_second, 3),
-        (y_third, 2), (y_third, 3),
-    ):
-        step(k)
-    every(z_third)
+    for step, k in STEPS:
+        {"M": multiply, "N": y_near, "S": y_second, "Y": y_third, "Z": z_second, "A": z_third}[step](k)
     tile = peaks[0]
     for more in peaks[1:]:
         tile = jnp.maximum(tile, more)
     peak_sent = peak_start(1, 0, tile)
-    act_z_end(0)
+    ended = [k for step, k in STEPS if step == "A"]
+    act_z_end(ended[0])
     tile = peak_end(1, 0, peak_sent, tile)
+    peak_sent = peak_start(1, 2, tile)
+    for k in ended[1:]:
+        act_z_end(k)
+    tile = peak_end(1, 2, peak_sent, tile)
     peak_sent = peak_start(1, 1, tile)
-    for k in range(1, len(PIECES)):
-        act_z_end(k)
+    every(act_y_end)
     tile = peak_end(1, 1, peak_sent, tile)
-    peak_sent = peak_start(1, 2, tile)
-    every(act_y_end)
-    tile = peak_end(1, 2, peak_sent, tile)
     level, inverse = levels(tile, 0.125)
 
     def saturated(values):
@@ -368,8 +405,12 @@
             lanes = slice(256 * n + 128 * half, 256 * n + 128 * half + 128)
             out[:, lanes] = (token_pad[0:12, lanes] + total[0:12, :]).astype(BF16)
 
-    for step in (down_multiply, down_x_first, down_l_first, down_last):
-        every(step, 3)
+    for step, n in (
+        (down_multiply, 0), (down_multiply, 1), (down_x_first, 0), (down_multiply, 2),
+        (down_x_first, 1), (down_x_first, 2), (down_l_first, 0), (down_l_first, 1),
+        (down_l_first, 2), (down_last, 0), (down_last, 1), (down_last, 2),
+    ):
+        step(n)
 
     for copy in copies:
         copy.wait_send()
@@ -410,8 +451,8 @@
             vmem((3, 4, 2, 16, 128), F32),
             vmem((3, 4, 2, 16, 128), BF16),
             vmem((3, 4, 2, 16, 128), BF16),
-            vmem((6, 8, 128), F32),
-            vmem((6, 15, 8, 128), F32),
+            vmem((6, 1, 128), F32),
+            vmem((6, 15, 1, 128), F32),
             pltpu.SemaphoreType.DMA((MAX_COPIES,)),
             pltpu.SemaphoreType.DMA((MAX_COPIES,)),
             pltpu.SemaphoreType.DMA((4,)),

time: 95.7 us -> 88.9 us (0.929)
  Pallas kernels: 94.1 us -> 87.4 us
    pallas_call x1, Pallas kernels: 94.1 us -> 87.4 us  [on_device(): pl.pallas_call(kernel, out_shape=jax.ShapeDtypeStruct((12, 768), BF16), i...]
where the time goes in v3:
time: 88.9 us; the launch traced here: 88.7 us
  Pallas kernels  87.4 us (98%)
  local copies, waits for them, and re-layouts  1.35 us (2%)
    pallas_call x1, Pallas kernels, on_device(): pl.pallas_call(kernel, out_shape=jax.ShapeDtypeStruct((12, 768), BF16), i...  87.4 us

profile of v3, /device:TPU:1, one launch (start us, length us, event | category | flops | bytes accessed | tf_op | source)
XLA Modules:
  0.0 88.7 jit_solution(2517244002540296717)
XLA Ops:
  0.0 87.4 %swiglu_block.1 = bf16[12,768]{1,0:T(8,128)(2,1)} custom-call(bf16[12,768]{1,0:T(8,128)(2,1)} %tokens.1, bf16[768,896]{1,0:T(8,128)(2,1)} %gate_hbm.1, bf16[768,896]{1,0:T(8,128)(2,1)} %up_hbm.1, bf16[896,768]{1,0:T(8,128)(2,1)} %down_hbm.1), custom_call_target="tpu_custom_call" | custom-call | flops 1585446912 | bytes 4128768 | tf_op jit(solution)/shard_map/swiglu_block/pallas_call | solution.py:421
  87.4 1.3 %copy.6 = bf16[12,768]{1,0:T(8,128)(2,1)} copy(bf16[12,768]{1,0:T(8,128)(2,1)} %swiglu_block.1) | data formatting | bytes 36864

commit v4 on v3

--- a/solution.py
+++ b/solution.py
@@ -10,10 +10,11 @@
 
 PIECES = ((6, 1), (0, 2), (2, 2), (4, 2))
 Y_RING = (False, True, True, True)
-Z_RING = (False, True, True, False)
+Z_RING = (False, True, True, True)
 STEPS = [(name[0], int(name[1])) for name in (
     "M0", "M1", "M2", "M3", "N1", "N2", "S1", "S2", "N3", "Y0",
-    "S3", "Y1", "Y2", "Y3", "A0", "Z1", "Z2", "A3", "A1", "A2",
+    "S3", "Y1", "Y2", "P1", "Y3", "P2", "P3", "A0", "Z1", "Z2",
+    "Z3", "A1", "A2", "A3",
 )]
 Z_ORDER = sorted(range(1, 16), key=lambda o: -min(o, 16 - o))
 PLANE_ORDER = sorted(range(1, 16), key=lambda o: abs(o // 4 - 2) + abs(o % 4 - 2))
@@ -44,7 +45,7 @@
     tokens, gate_hbm, up_hbm, down_hbm, out,
     gate_w, up_w, down_w, token_in, token_pad, token_z, token_f, token_x, scaled,
     keep, y_send, y_recv, z_sum, z_sum1, z_send, z_recv, act, act1, scaled_act,
-    down_part, core_send, core_recv, x_send, x_recv, l_own, l_send, l_recv,
+    down_total, down_part, core_send, core_recv, x_send, x_recv, l_own, l_send, l_recv,
     peak_send, peak_recv, send_sem, recv_sem, load_sem,
 ):
     width, hidden = lax.axis_index("width"), lax.axis_index("hidden")
@@ -254,9 +255,9 @@
             z_sum1[:, 96:128, :] = jnp.zeros((2, 32, 128), F32)
         rows = z_rows(k)
         if Z_RING[k]:
-            for m, g, j in ((0, 0, 2), (1, 1, 2), (2, 1, 1), (3, 0, 3)):
-                z_send[k, m // 2, m % 2, 0:rows, :] = z_read(k, g, ring_add(j, zh)).astype(BF16)
-            state[k]["z"] = z_ring(k, range(4))
+            for m in range(2):
+                z_send[k, 0, m, 0:rows, :] = z_read(k, m, ring_add(2, zh)).astype(BF16)
+            state[k]["z"] = z_ring(k, (0, 1))
             return
         state[k]["z"] = []
         for o in (2, 1, 3):
@@ -270,6 +271,12 @@
                 )
             )
 
+    def z_near(k):
+        rows = z_rows(k)
+        z_send[k, 1, 0, 0:rows, :] = z_read(k, 1, ring_add(1, zh)).astype(BF16)
+        z_send[k, 1, 1, 0:rows, :] = z_read(k, 0, ring_add(3, zh)).astype(BF16)
+        state[k]["z"].update(z_ring(k, (2, 3)))
+
     def z_slot(ref, k, m):
         return ref.at[k, m // 2, m % 2, pl.ds(0, z_rows(k))]
 
@@ -308,17 +315,22 @@
         peaks.append(fold_max(value))
         mine = act_ref(k, y, zh)
         mine[...] = value.astype(BF16)
-        state[k]["az"] = [send(mine, mine, along("zh", o)) for o in (2, 1, 3)]
-
-    def act_z_end(k):
-        for copy in state[k]["az"]:
-            copy.wait_recv()
-        first, count = PIECES[k]
-        if count == 2:
-            mine = act.at[pl.ds(first, 2), pl.ds(pl.multiple_of(y * 96, 96), 96), :]
-        else:
-            mine = act1.at[y, pl.ds(0, 96), :]
-        state[k]["ay"] = [send(mine, mine, along("y", o)) for o in (2, 1, 3)]
+        state[k]["az"] = {o: send(mine, mine, along("zh", o)) for o in (2, 1, 3)}
+        state[k]["ay"] = []
+        pass_on(k, 0)
+
+    def pass_on(k, o):
+        block = act_ref(k, y, ring_add(4 - o, zh))
+        state[k]["ay"] += [send(block, block, along("y", place)) for place in (2, 1, 3)]
+
+    def act_near(k):
+        for o in (1, 3):
+            state[k]["az"][o].wait_recv()
+            pass_on(k, o)
+
+    def act_far(k):
+        state[k]["az"][2].wait_recv()
+        pass_on(k, 2)
 
     def act_y_end(k):
         for copy in state[k]["ay"]:
@@ -329,38 +341,62 @@
             step(k)
 
     for step, k in STEPS:
-        {"M": multiply, "N": y_near, "S": y_second, "Y": y_third, "Z": z_second, "A": z_third}[step](k)
+        {"M": multiply, "N": y_near, "P": z_near, "S": y_second, "Y": y_third, "Z": z_second, "A": z_third}[step](k)
     tile = peaks[0]
     for more in peaks[1:]:
         tile = jnp.maximum(tile, more)
     peak_sent = peak_start(1, 0, tile)
     ended = [k for step, k in STEPS if step == "A"]
-    act_z_end(ended[0])
+    act_near(ended[0])
     tile = peak_end(1, 0, peak_sent, tile)
+    peak_sent = peak_start(1, 1, tile)
+    for k in ended[1:]:
+        act_near(k)
+    for k in ended[:-1]:
+        act_far(k)
+    tile = peak_end(1, 1, peak_sent, tile)
     peak_sent = peak_start(1, 2, tile)
-    for k in ended[1:]:
-        act_z_end(k)
+    act_far(ended[-1])
     tile = peak_end(1, 2, peak_sent, tile)
-    peak_sent = peak_start(1, 1, tile)
-    every(act_y_end)
-    tile = peak_end(1, 1, peak_sent, tile)
     level, inverse = levels(tile, 0.125)
 
     def saturated(values):
         return (level * jnp.tanh(values.astype(F32) * inverse)).astype(BF16)
 
-    for t in range(6):
-        scaled_act[:, 128 * t : 128 * t + 128] = saturated(act[t])
-    for d in range(4):
-        scaled_act[96 * d : 96 * d + 96, 768:896] = saturated(act1[d, 0:96, :])
+    def piece_columns(k):
+        first, count = PIECES[k]
+        return slice(128 * first, 128 * (first + count))
+
+    def saturate_piece(k):
+        first, count = PIECES[k]
+        if count == 1:
+            for d in range(4):
+                scaled_act[96 * d : 96 * d + 96, 768:896] = saturated(act1[d, 0:96, :])
+            return
+        for t in range(first, first + count):
+            scaled_act[:, 128 * t : 128 * t + 128] = saturated(act[t])
 
     loads[2].wait()
+    for at, k in enumerate(ended):
+        act_y_end(k)
+        saturate_piece(k)
+        if at < len(ended) - 1:
+            part = jnp.dot(
+                scaled_act[:, piece_columns(k)], down_w[piece_columns(k), :],
+                preferred_element_type=F32,
+            )
+            if at == 0:
+                down_total[...] = part
+            else:
+                down_total[...] += part
 
     downs = [dict() for _ in range(3)]
 
     def down_multiply(n):
-        result = jnp.dot(
-            scaled_act[...], down_w[:, 256 * n : 256 * n + 256], preferred_element_type=F32
+        columns = slice(256 * n, 256 * n + 256)
+        last = piece_columns(ended[-1])
+        result = down_total[:, columns] + jnp.dot(
+            scaled_act[:, last], down_w[last, columns], preferred_element_type=F32
         )
         for half in range(2):
             for d in range(4):
@@ -443,6 +479,7 @@
             vmem((6, 384, 128), BF16),
             vmem((4, 128, 128), BF16),
             vmem((384, 896), BF16),
+            vmem((384, 768), F32),
             vmem((3, 2, 2, 4, 48, 128), F32),
             vmem((3, 2, 4, 48, 128), BF16),
             vmem((3, 2, 4, 48, 128), BF16),

time: 88.9 us -> 87.4 us (0.983)
  Pallas kernels: 87.4 us -> 85.9 us
    pallas_call x1, Pallas kernels: 87.4 us -> 85.9 us  [on_device(): pl.pallas_call(kernel, out_shape=jax.ShapeDtypeStruct((12, 768), BF16), i...]
where the time goes in v4:
time: 87.4 us; the launch traced here: 87.2 us
  Pallas kernels  85.9 us (98%)
  local copies, waits for them, and re-layouts  1.35 us (2%)
    pallas_call x1, Pallas kernels, on_device(): pl.pallas_call(kernel, out_shape=jax.ShapeDtypeStruct((12, 768), BF16), i...  85.9 us

profile of v4, /device:TPU:1, one launch (start us, length us, event | category | flops | bytes accessed | tf_op | source)
XLA Modules:
  0.0 87.2 jit_solution(15043040832366135464)
XLA Ops:
  0.0 85.9 %swiglu_block.1 = bf16[12,768]{1,0:T(8,128)(2,1)} custom-call(bf16[12,768]{1,0:T(8,128)(2,1)} %tokens.1, bf16[768,896]{1,0:T(8,128)(2,1)} %gate_hbm.1, bf16[768,896]{1,0:T(8,128)(2,1)} %up_hbm.1, bf16[896,768]{1,0:T(8,128)(2,1)} %down_hbm.1), custom_call_target="tpu_custom_call" | custom-call | flops 1585446912 | bytes 4128768 | tf_op jit(solution)/shard_map/swiglu_block/pallas_call | solution.py:457
  85.9 1.3 %copy.6 = bf16[12,768]{1,0:T(8,128)(2,1)} copy(bf16[12,768]{1,0:T(8,128)(2,1)} %swiglu_block.1) | data formatting | bytes 36864

commit v5 on v4

--- a/solution.py
+++ b/solution.py
@@ -12,7 +12,7 @@
 Y_RING = (False, True, True, True)
 Z_RING = (False, True, True, True)
 STEPS = [(name[0], int(name[1])) for name in (
-    "M0", "M1", "M2", "M3", "N1", "N2", "S1", "S2", "N3", "Y0",
+    "M1", "M0", "M2", "M3", "N1", "N2", "S1", "S2", "N3", "Y0",
     "S3", "Y1", "Y2", "P1", "Y3", "P2", "P3", "A0", "Z1", "Z2",
     "Z3", "A1", "A2", "A3",
 )]

time: 87.4 us -> 87.5 us (level)
  no operation moved by 1% of the time
where the time goes in v5:
time: 87.5 us; the launch traced here: 87.4 us
  Pallas kernels  86 us (98%)
  local copies, waits for them, and re-layouts  1.35 us (2%)
    pallas_call x1, Pallas kernels, on_device(): pl.pallas_call(kernel, out_shape=jax.ShapeDtypeStruct((12, 768), BF16), i...  86 us

profile of v5, /device:TPU:1, one launch (start us, length us, event | category | flops | bytes accessed | tf_op | source)
XLA Modules:
  0.0 87.4 jit_solution(8608371784093367372)
XLA Ops:
  0.0 86.0 %swiglu_block.1 = bf16[12,768]{1,0:T(8,128)(2,1)} custom-call(bf16[12,768]{1,0:T(8,128)(2,1)} %tokens.1, bf16[768,896]{1,0:T(8,128)(2,1)} %gate_hbm.1, bf16[768,896]{1,0:T(8,128)(2,1)} %up_hbm.1, bf16[896,768]{1,0:T(8,128)(2,1)} %down_hbm.1), custom_call_target="tpu_custom_call" | custom-call | flops 1585446912 | bytes 4128768 | tf_op jit(solution)/shard_map/swiglu_block/pallas_call | solution.py:457
  86.0 1.3 %copy.6 = bf16[12,768]{1,0:T(8,128)(2,1)} copy(bf16[12,768]{1,0:T(8,128)(2,1)} %swiglu_block.1) | data formatting | bytes 36864
